TPU v7x, 32 devices: a whole 2x2x4 slice. The times are simulated.
32 devices in a mesh: dp: 8 (over z, y), sub: 4 (over x, core).
Axes of the slice: x: 2, y: 2, z: 4, core: 2. Of those that a mesh axis runs over, the one named last changes fastest.
Arguments:
- latents: float32 [64, 128, 768], P(('dp', 'sub')), may hold values from -6 to 6
- inputs: bfloat16 [64, 1024, 768], P(('dp', 'sub')), may hold values from -6 to 6
- counts: int32 [64], P(('dp', 'sub')), may hold values from 512 to 1024, as said below
- flags: int32 [2], replicated, may hold values from 0 to 1, as said below
- cross_attn: bfloat16 [768, 3072], P('dp', 'sub'), may hold values from -2.8 to 2.8
- cross_up: bfloat16 [768, 3072], P('dp', 'sub'), may hold values from -0.21875 to 0.21875
- cross_down: bfloat16 [3072, 768], P('dp', 'sub'), may hold values from -0.109375 to 0.109375
- self_attn: bfloat16 [768, 3072], P('dp', 'sub'), may hold values from -1 to 1
- self_up: bfloat16 [768, 3072], P('dp', 'sub'), may hold values from -0.21875 to 0.21875
- self_down: bfloat16 [3072, 768], P('dp', 'sub'), may hold values from -0.109375 to 0.109375
- gains: bfloat16 [5, 768], P(None, 'dp'), may hold values from 0.5 to 1.5
- cotangent: float32 [64, 128, 768], P(('dp', 'sub')), may hold values from -6 to 6
Outputs:
- latents_out: float32 [64, 128, 768], P(('dp', 'sub'))
- latents_grad: float32 [64, 128, 768], P(('dp', 'sub'))
- inputs_grad: float32 [64, 1024, 768], P(('dp', 'sub'))
- cross_attn_grad: float32 [768, 3072], P('dp', 'sub')
- cross_up_grad: float32 [768, 3072], P('dp', 'sub')
- cross_down_grad: float32 [3072, 768], P('dp', 'sub')
- self_attn_grad: float32 [768, 3072], P('dp', 'sub')
- self_up_grad: float32 [768, 3072], P('dp', 'sub')
- self_down_grad: float32 [3072, 768], P('dp', 'sub')
- gains_grad: float32 [5, 768], P(None, 'dp')
Inputs may be any that keep to these rules, and one draw needn't show every extreme that they name: `counts`: within each aligned group of 2 items one item has all 1024 slots live. `flags`: at least one step has flag 1 and at least one has flag 0.
All inputs are finite; a program needn't handle non-finite values.
Results may differ from a plain program's by a relative error of at most 0.019.
Values may be sent and summed in bfloat16 or wider, within the bound.
A program may use at most 256 MiB of HBM per device.

v0:
```python
import collections
import functools

import jax
import jax.numpy as jnp
from jax import lax
from jax.experimental import pallas as pl
from jax.experimental.pallas import tpu as pltpu
from jax.sharding import PartitionSpec as P

HEADS = 12
EPSILON = 1e-05
MASKED = -1e30
MESH_ID = pl.DeviceIdType.MESH
F32 = jnp.float32
BF16 = jnp.bfloat16
ANY = pl.BlockSpec(memory_space=pl.ANY)
VMEM = pl.BlockSpec(memory_space=pltpu.VMEM)
SMEM = pl.BlockSpec(memory_space=pltpu.SMEM)


PIECES = {
    "C": (0, 2),
    "A": (2, 1),
    "B": (3, 1),
    "D": (4, 2),
    "CA": (0, 3),
    "AB": (2, 2),
    "BD": (3, 3),
}


def piece(name, rows):
    first, size = PIECES[name]
    return pl.ds(first * (rows // 6), size * (rows // 6))


class Place:
    def __init__(self):
        dp, sub = lax.axis_index("dp"), lax.axis_index("sub")
        self.z, self.y, self.x, self.c = dp // 2, dp % 2, sub // 2, sub % 2

    def dev(self, z=None, y=None, x=None, c=None):
        z = self.z if z is None else z
        y = self.y if y is None else y
        x = self.x if x is None else x
        c = self.c if c is None else c
        return (z * 2 + y, x * 2 + c)

    def zk(self, k):
        return (self.z + k) % 4


def now(ref):
    return ref() if callable(ref) else ref


def spot(ref, index):
    return lambda: ref.at[index]


def only_if(condition, action):
    if condition is None:
        action()
    else:
        pl.when(condition())(action)


class Flight:
    def __init__(self, sems, ref, send_index, recv_index):
        self.sems, self.ref, self.send_index, self.recv_index = sems, ref, send_index, recv_index

    def made(self):
        place = self.sems.place
        return pltpu.make_async_remote_copy(
            src_ref=now(self.ref),
            dst_ref=now(self.ref),
            send_sem=self.sems.send.at[self.send_index],
            recv_sem=self.sems.recv.at[self.recv_index],
            device_id=place.dev(c=1 - place.c),
            device_id_type=MESH_ID,
        )

    def wait_send(self):
        self.made().wait_send()

    def wait_recv(self):
        self.made().wait_recv()


class Sems:
    def __init__(self, place, send, recv):
        self.place, self.send, self.recv, self.count, self.sent = place, send, recv, 0, []

    def reserve(self, n):
        self.count += n
        return self.count - n

    def start(self, src, dst, device, send_index, recv_index, condition=None, later=True):
        def action():
            pltpu.make_async_remote_copy(
                src_ref=now(src),
                dst_ref=now(dst),
                send_sem=self.send.at[send_index],
                recv_sem=self.recv.at[recv_index],
                device_id=device,
                device_id_type=MESH_ID,
            ).start()

        only_if(condition, action)
        flight = Flight(self, dst, send_index, recv_index)
        if later:
            self.sent.append((condition, flight))
        return flight

    def copy(self, src, dst, device, later=True):
        index = self.reserve(1)
        return self.start(src, dst, device, index, index, later=later)

    def drain(self):
        for condition, flight in self.sent:
            only_if(condition, flight.wait_send)


def greet(place, devices):
    barrier = pltpu.get_barrier_semaphore()
    for device in devices:
        pl.semaphore_signal(barrier, inc=1, device_id=device, device_id_type=MESH_ID)
    pl.semaphore_wait(barrier, len(devices))


def wait_all(copies):
    for made in copies:
        made.wait_recv()


class Spread:
    def __init__(self, sems, src, where):
        self.sems, self.where, place = sems, where, sems.place
        self.base = sems.reserve(4)
        z = place.z
        for k, condition in ((1, lambda: z != 3), (2, None), (3, lambda: z != 0)):
            at = self.base + k - 1
            sems.start(src, where(z), place.dev(z=place.zk(k)), at, at, condition)

    def arrived(self, k):
        origin = self.sems.place.zk(4 - k)
        Flight(self.sems, self.where(origin), self.base + 3, self.base + k - 1).wait_recv()

    def forward(self):
        self.arrived(2)
        place = self.sems.place
        block = self.where(place.zk(2))
        for z, target, k in ((2, 3, 3), (1, 0, 1)):
            self.sems.start(
                block,
                block,
                place.dev(z=target),
                self.base + 3,
                self.base + k - 1,
                functools.partial(lambda z: place.z == z, z),
            )

    def finish(self):
        self.arrived(1)
        self.arrived(3)


class Collect:
    def __init__(self, sems, part, into, through):
        self.sems, self.part, self.into, self.through = sems, part, into, through
        place = sems.place
        self.base = sems.reserve(4)
        z = place.z
        for k, condition in (
            (1, lambda: z != 3),
            (2, lambda: (z == 0) | (z == 3)),
            (3, lambda: z != 0),
        ):
            self.send(k, condition)
        for k, end, middle in ((1, 3, 2), (3, 0, 1)):
            at = self.base + 3
            sems.start(part(place.zk(k)), through, place.dev(z=middle), at, at, functools.partial(lambda end: z == end, end))

    def send(self, k, condition):
        place, at = self.sems.place, self.base + k - 1
        self.sems.start(
            self.part(place.zk(k)),
            spot(self.into, k - 1),
            place.dev(z=place.zk(k)),
            at,
            at,
            condition,
        )

    def forward(self, add):
        place = self.sems.place

        def middle():
            return (place.z == 1) | (place.z == 2)

        @pl.when(middle())
        def _():
            Flight(self.sems, self.through, self.base + 3, self.base + 3).wait_recv()
            add(place.zk(2))

        self.send(2, middle)

    def finish(self):
        z = self.sems.place.z
        for k, condition in ((1, lambda: z != 0), (2, None), (3, lambda: z != 3)):
            flight = Flight(self.sems, spot(self.into, k - 1), self.base + 3, self.base + k - 1)
            only_if(condition, flight.wait_recv)


def slots(count, places, order):
    steps = []
    for slot in range(min(places.values()), count + max(places.values())):
        for name in order:
            i = slot - places[name]
            if 0 <= i < count:
                steps.append((slot, name, i))
    return steps


def dot(a, b):
    return jnp.dot(a, b, preferred_element_type=F32)


def dot_nt(a, b):
    return lax.dot_general(a, b, (((1,), (1,)), ((), ())), preferred_element_type=F32)


def low(values):
    return values.astype(BF16)


def normed(values):
    centred = values - jnp.mean(values, axis=-1, keepdims=True)
    inverse = lax.rsqrt(jnp.mean(centred * centred, axis=-1, keepdims=True) + EPSILON)
    return centred * inverse, inverse


def gelu_both(u):
    k, a = 0.7978845608028654, 0.044715
    square = u * u
    t = jnp.tanh(k * u * (1.0 + a * square))
    half = 0.5 * (1.0 + t)
    slope = half + (0.5 * k) * u * (1.0 - t * t) * (1.0 + (3.0 * a) * square)
    return u * half, slope


def square_block(ref, x, c):
    halves = []
    for h in range(2):
        block = ref[h, x, c]
        halves.append(block.reshape(-1, block.shape[3]))
    return jnp.concatenate(halves, axis=1)


def hidden_block(ref, z):
    parts = []
    for y in range(2):
        rows = [ref[h, x, c, z, y] for x in range(2) for c in range(2) for h in range(2)]
        parts.append(jnp.concatenate(rows, axis=0))
    return jnp.concatenate(parts, axis=1)


def left_half(shape):
    return lax.broadcasted_iota(jnp.int32, shape, 1) < 64


def stack_heads(values):
    left = left_half(values.shape)
    zero = jnp.zeros_like(values)
    return jnp.concatenate([jnp.where(left, values, zero), jnp.where(left, zero, values)], axis=0)


def join_heads(values):
    rows = values.shape[0] // 2
    top, bottom = values[:rows], values[rows:]
    return jnp.where(left_half(top.shape), top, bottom)


def lanes(index, size):
    return pl.ds(pl.multiple_of(index * size, size), size)


def kept_shapes(rows, tokens, width, hidden):
    two = 2 * rows
    return {
        "cq": ((rows, width), BF16),
        "kv": ((2, tokens, width), BF16),
        "cp": ((width // 128, two, tokens), BF16),
        "co": ((rows, width), F32),
        "mid": ((rows, width), F32),
        "gpc": ((rows, hidden), BF16),
        "ac": ((two, width), F32),
        "sqkv": ((3, two, width), BF16),
        "sp": ((2 * (width // 128), two, rows), BF16),
        "aa": ((two, width), F32),
        "gps": ((two, hidden), BF16),
        "xl": ((tokens, width), BF16),
    }


def paired_shapes(rows, tokens, width, hidden):
    two = 2 * rows
    return {
        "gyt": ((2, width // 4, 2 * two), BF16),
        "mh": ((2 * two, hidden), BF16),
        "mnt": ((width, 2 * two), BF16),
        "sbt": ((width, 2 * two), BF16),
        "l1t": ((width, 2 * two), BF16),
        "ch": ((two, hidden), BF16),
        "cnt": ((width, two), BF16),
        "lst": ((width, two), BF16),
        "xbt": ((width, 2 * tokens), BF16),
    }


def forward_kernel(names, dims, *refs):
    rows, tokens, width, hidden = dims
    two = 2 * rows
    count = 6
    refs = list(refs)

    def take(n):
        out = refs[:n]
        del refs[:n]
        return out

    own = take(count)
    gain, lat, tok, cot, live_counts, flags = take(6)
    full = take(count)
    gain_out, result = take(2)
    kept = dict(zip(names, take(len(names))))
    gain_all, lat_v, cot_v, tok_v, z2, xb, xbt, gyt, lst, wr0, wr1, wt = take(12)
    cq, kv, cp, co, mid, ch, gpc, ac, sqkv, sp, so, aa, mh, gps, xl, lt, cnt, mnt = take(18)
    gain_own, gain_one, zb_v, nb = take(4)
    send, recv, local = take(3)
    wr = (wr0, wr1)
    place = Place()
    x, y, z, c = place.x, place.y, place.z, place.c
    sems = Sems(place, send, recv)
    local_count = [0]
    local_open = []

    def local_copy(src, dst):
        made = pltpu.make_async_copy(src, dst, local.at[local_count[0]])
        local_count[0] += 1
        made.start()
        return made

    in_gain = local_copy(gain, gain_own)
    in_lat, in_tok, in_cot = local_copy(lat, lat_v), local_copy(tok, tok_v), local_copy(cot, cot_v)
    px, py, pc = place.dev(x=1 - x), place.dev(y=1 - y), place.dev(c=1 - c)
    me_dp = z * 2 + y
    dp_peers = [((me_dp + k) % 8, x * 2 + c) for k in range(1, 8)]
    greet(place, dp_peers + [px, pc])

    halves = 2 * count
    blocks = [full[i // 2].at[i % 2] for i in range(halves)]
    ones, twos, threes, across, placed = {}, {}, {}, {i: [] for i in range(halves)}, {}
    block_rows = full[0].shape[5]

    def shard(i):
        w, h = own[i // 2], i % 2
        if w.shape[0] == block_rows:
            return w, slice(None), pl.ds(h * (w.shape[1] // 2), w.shape[1] // 2), 0
        return w, slice(None), pl.ds(0, w.shape[1]), h * block_rows

    def own_piece(i, name):
        w, unused, columns, first = shard(i)
        at = piece(name, block_rows)
        return w.at[pl.ds(first + at.start, at.size), columns]

    def step_one(i):
        g = blocks[i]
        w, unused, columns, first = shard(i)
        placed[i] = local_copy(w.at[pl.ds(first, block_rows), columns], g.at[x, c, z, y])
        ab, pc_, pd = (piece(n, block_rows) for n in ("AB", "C", "D"))
        spread = Spread(sems, own_piece(i, "AB"), lambda o: g.at[x, c, o, y, ab])
        ones[i] = (
            spread,
            [
                sems.copy(own_piece(i, "C"), g.at[x, c, z, y, pc_], px),
                sems.copy(own_piece(i, "D"), g.at[x, c, z, y, pd], py),
            ],
        )

    def step_one_forward(i):
        ones[i][0].forward()

    def step_two(i):
        g = blocks[i]
        spread, got = ones.pop(i)
        placed.pop(i).wait()
        wait_all(got)
        pa, pb, pc_, pd = (piece(n, block_rows) for n in ("A", "B", "C", "D"))
        spread_c = Spread(sems, g.at[:, c, z, y, pc_], lambda o: g.at[:, c, o, y, pc_])
        spread_d = Spread(sems, g.at[x, c, z, :, pd], lambda o: g.at[x, c, o, :, pd])
        spread.finish()
        got = [
            sems.copy(g.at[x, c, :, y, pa], g.at[x, c, :, y, pa], px),
            sems.copy(g.at[x, c, :, y, pb], g.at[x, c, :, y, pb], py),
        ]
        twos[i] = ((spread_c, spread_d), got)

    def step_two_forward(i):
        for spread in twos[i][0]:
            spread.forward()

    def step_three(i):
        g = blocks[i]
        spreads, got = twos.pop(i)
        for spread in spreads:
            spread.finish()
        wait_all(got)
        ca, bd = piece("CA", block_rows), piece("BD", block_rows)
        threes[i] = [
            sems.copy(g.at[:, c, :, y, ca], g.at[:, c, :, y, ca], py),
            sems.copy(g.at[x, c, :, :, bd], g.at[x, c, :, :, bd], px),
        ]
        across[i] += [
            sems.copy(g.at[:, c, :, y, ca], g.at[:, c, :, y, ca], pc),
            sems.copy(g.at[x, c, :, :, bd], g.at[x, c, :, :, bd], pc),
        ]

    def step_four(i):
        wait_all(threes.pop(i))
        g = blocks[i]
        ca, bd = piece("CA", block_rows), piece("BD", block_rows)
        across[i] += [
            sems.copy(g.at[:, c, :, 1 - y, ca], g.at[:, c, :, 1 - y, ca], pc),
            sems.copy(g.at[1 - x, c, :, :, bd], g.at[1 - x, c, :, :, bd], pc),
        ]

    loading = {}

    def load(m, dst):
        def begin():
            for h in range(2):
                wait_all(across.pop(2 * m + h))
            loading[m] = local_copy(full[m], dst)

        return begin

    def keep(name, src):
        local_open.append(local_copy(src, kept[name]))

    def pair(name, mine, theirs, axis_size, axis):
        here, there = pl.ds(0, axis_size), pl.ds(axis_size, axis_size)
        dst = kept[name]

        def part(where):
            return dst.at[where] if axis == 0 else dst.at[:, where] if axis == 1 else dst.at[:, :, where]

        local_open.append(local_copy(mine, part(here)))
        across_pairs.append(sems.copy(theirs, part(there), pc))

    across_pairs = []
    gain_copies = []

    def pick(flag_first, first, second):
        return jnp.where(flag_first, first, second)

    first_live = flags[0] == 0
    live_count = jnp.where(first_live, live_counts[0], live_counts[1])

    def send_gains():
        in_gain.wait()
        gain_one[...] = jnp.zeros_like(gain_one)
        gain_one[: gain.shape[0], : gain.shape[1]] = gain_own[...]
        gain_all[me_dp] = gain_one[...]
        for device in dp_peers:
            gain_copies.append(sems.copy(gain_one, gain_all.at[me_dp], device))

    def start():
        wait_all(gain_copies)
        row = lax.broadcasted_iota(jnp.int32, (128, width), 0)
        column = lax.broadcasted_iota(jnp.int32, (128, width), 1)
        share = width // 8
        gain_out[...] = jnp.zeros_like(gain_out)

        @pl.loop(0, 8)
        def _(i):
            spread = low(jnp.where((column == row + share * i) & (row < share), 1.0, 0.0))
            gain_out[...] += dot(gain_all[i], spread)

        in_lat.wait()
        in_cot.wait()
        z2[:rows] = pick(first_live, lat_v[0], lat_v[1])
        z2[rows:] = pick(first_live, lat_v[1], lat_v[0])
        zb = low(normed(z2[:rows])[0] * gain_out[0:1])
        zb_v[...] = zb
        lst[0] = zb.T
        gy_first = low(pick(first_live, cot_v[0], cot_v[1]))
        gy_last = low(pick(first_live, cot_v[1], cot_v[0]))
        gyt[:, :, :, :rows] = gy_first.T.reshape(2, 2, width // 4, rows)
        gyt[:, :, :, rows:] = gy_last.T.reshape(2, 2, width // 4, rows)
        pair("gyt", gyt.at[:, c], gyt.at[:, 1 - c], two, 2)

    def tokens_part(first, last):
        def run():
            if first == 0:
                in_tok.wait()

            @pl.loop(first, last)
            def _(i):
                at = lanes(i, 128)
                here = pick(first_live, tok_v[0, at], tok_v[1, at])
                xl[at] = here
                value = low(normed(here.astype(F32))[0] * gain_out[1:2])
                xb[at] = value
                xbt[:, at] = value.T

            if last == tokens // 128:
                keep("xl", xl)
                pair("xbt", xbt, xbt, tokens, 1)

        return run

    def cross_queries():
        loading[0].wait()
        cq[...] = low(dot(zb_v[...], square_block(wr[0], 0, 0)))
        keep("cq", cq)

    def keys_values(first, last):
        def run():
            for i in range(first, last):
                at = pl.ds(i * 256, 256)

                @pl.loop(0, 2)
                def _(j):
                    kv[j, at] = low(dot(xb[at], square_block(wr[0], j, 1 - j)))

            if last == tokens // 256:
                keep("kv", kv)

        return run

    def cross_attention(first, last):
        def run():
            @pl.loop(first, last)
            def _(p):
                at = lanes(p, 128)
                q = stack_heads(cq[:, at] * jnp.asarray(0.125, BF16))
                s = dot_nt(q, kv[0, :, at])
                s = jnp.where(lax.broadcasted_iota(jnp.int32, s.shape, 1) < live_count, s, MASKED)
                e = jnp.exp(s - jnp.max(s, axis=-1, keepdims=True))
                prob = low(e * (1.0 / jnp.sum(e, axis=-1, keepdims=True)))
                cp[p] = prob
                co[:, at] = join_heads(dot(prob, kv[1, :, at]))

            if last == width // 128:
                keep("cp", cp)
                keep("co", co)

        return run

    def cross_out():
        cob = low(co[...])
        lst[1] = cob.T
        pair("lst", lst.at[c], lst.at[1 - c], rows, 1)
        mid[...] = z2[:rows] + dot(cob, square_block(wr[0], 1, 1))
        keep("mid", mid)
        cnb = low(normed(mid[...])[0] * gain_out[2:3])
        nb[:rows] = cnb
        cnt[...] = cnb.T
        pair("cnt", cnt, cnt, rows, 1)

    def up(m, w, left, out, slope, first, last, after):
        def run():
            if first == 0:
                loading[m].wait()

            @pl.loop(first, last)
            def _(s):
                at = lanes(s, hidden // 4)
                value, grad = gelu_both(dot(nb[:left], square_block(w, s // 2, s % 2)))
                out[:, at] = low(value)
                slope[:, at] = low(grad)

            if last == 4:
                after()

        return run

    def down(m, act, into):
        loading[m].wait()

        @pl.loop(0, 4)
        def _(s):
            into[...] += dot_nt(act[:, lanes(s, hidden // 4)], hidden_block(wt, s))

    def cross_up_done():
        pair("ch", ch, ch, rows, 0)
        keep("gpc", gpc)

    def self_up_done():
        pair("mh", mh, mh, two, 0)
        keep("gps", gps)

    def cross_down():
        ac[:rows] = mid[...]
        ac[rows:] = z2[rows:]
        down(2, ch, ac.at[pl.ds(0, rows)])
        keep("ac", ac)
        sb = low(normed(ac[...])[0] * gain_out[3:4])
        nb[...] = sb
        lt[0] = sb.T
        pair("sbt", lt.at[0], lt.at[0], two, 1)

    def self_project():
        loading[3].wait()
        @pl.loop(0, 3)
        def _(i):
            sqkv[i] = low(dot(nb[...], square_block(wr[0], i // 2, i % 2)))

        keep("sqkv", sqkv)

    def self_attention(first, last):
        pairs = width // 128

        def run():
            @pl.loop(first, last, unroll=3)
            def _(i):
                at, row_at = lanes(i % pairs, 128), lanes(i // pairs, rows)
                q = stack_heads(sqkv[0, row_at, at] * jnp.asarray(0.125, BF16))
                s = dot_nt(q, sqkv[1, row_at, at])
                e = jnp.exp(s - jnp.max(s, axis=-1, keepdims=True))
                prob = low(e * (1.0 / jnp.sum(e, axis=-1, keepdims=True)))
                sp[i] = prob
                so[row_at, at] = low(join_heads(dot(prob, sqkv[2, row_at, at])))

            if last == 2 * pairs:
                keep("sp", sp)

        return run

    def self_out():
        lt[1] = so[...].T
        pair("l1t", lt.at[c], lt.at[1 - c], two, 1)
        aa[...] = ac[...] + dot(so[...], square_block(wr[0], 1, 1))
        keep("aa", aa)
        mnb = low(normed(aa[...])[0] * gain_out[4:5])
        nb[...] = mnb
        mnt[...] = mnb.T
        pair("mnt", mnt, mnt, two, 1)

    def self_down():
        z2[...] = aa[...]
        down(5, mh, z2)
        total = z2[...]
        result[0] = pick(first_live, total[:rows], total[rows:])
        result[1] = pick(first_live, total[rows:], total[:rows])

    pairs = width // 128
    work = collections.deque([(-2, send_gains), (1, start)])
    for n in range(4):
        work.append((1, tokens_part(n * tokens // 512, (n + 1) * tokens // 512)))
    for slot, part in (
        (4, load(0, wr[0])),
        (4, cross_queries),
        (4, keys_values(0, 1)),
        (4, keys_values(1, 2)),
        (4, keys_values(2, 3)),
        (4, keys_values(3, tokens // 256)),
        (4, cross_attention(0, 2)),
        (4, cross_attention(2, 4)),
        (4, cross_attention(4, pairs)),
        (4, cross_out),
        (6, load(1, wr[1])),
        (6, up(1, wr[1], rows, ch, gpc, 0, 2, cross_up_done)),
        (6, up(1, wr[1], rows, ch, gpc, 2, 4, cross_up_done)),
        (8, load(2, wt)),
        (8, cross_down),
        (10, load(3, wr[0])),
        (10, self_project),
        (10, self_attention(0, pairs)),
        (10, self_attention(pairs, 2 * pairs)),
        (10, self_out),
        (12, load(4, wr[1])),
        (12, up(4, wr[1], two, mh, gps, 0, 2, self_up_done)),
        (12, up(4, wr[1], two, mh, gps, 2, 4, self_up_done)),
        (14, load(5, wt)),
        (14, self_down),
    ):
        work.append((slot, part))
    steps = {
        "1": step_one,
        "f": step_one_forward,
        "2": step_two,
        "g": step_two_forward,
        "3": step_three,
        "4": step_four,
    }
    places = {"1": -2, "f": -1, "2": 0, "g": 0, "3": 1, "4": 2}
    for slot, name, i in slots(halves, places, "231fg4"):
        steps[name](i)
        if work and work[0][0] <= slot:
            work.popleft()[1]()
    while work:
        work.popleft()[1]()
    wait_all(across_pairs)
    for made in local_open:
        made.wait()
    sems.drain()


def half_shape(shard):
    return shard.shape[0], shard.shape[1] // 2


def forward_all(own, gain, latents, inputs, cotangent, counts, flags):
    count = len(own)
    rows, width = latents.shape[1:]
    tokens = inputs.shape[1]
    hidden = own[1].shape[1] * 4
    dims = (rows, tokens, width, hidden)
    two = 2 * rows
    kept = {**kept_shapes(*dims), **paired_shapes(*dims)}
    names = tuple(kept)
    copies = 7 + 2 * count * (6 + 10 + 4 + 2) + len(paired_shapes(*dims))
    block = (2, 2, 2, 4, 2) + half_shape(own[0])
    shapes = [jax.ShapeDtypeStruct(block, BF16) for w in own]
    shapes += [
        jax.ShapeDtypeStruct((16, width), F32),
        jax.ShapeDtypeStruct(latents.shape, F32),
    ]
    shapes += [jax.ShapeDtypeStruct(s, t) for s, t in kept.values()]
    pairs = width // 128
    scratch = [
        ((8, 16, 128), BF16),
        (latents.shape, F32),
        (latents.shape, F32),
        (inputs.shape, BF16),
        ((two, width), F32),
        ((tokens, width), BF16),
        ((width, tokens), BF16),
        ((2, 2, width // 4, two), BF16),
        ((2, width, rows), BF16),
        (block, BF16),
        (block, BF16),
        (block, BF16),
        ((rows, width), BF16),
        ((2, tokens, width), BF16),
        ((pairs, two, tokens), BF16),
        ((rows, width), F32),
        ((rows, width), F32),
        ((rows, hidden), BF16),
        ((rows, hidden), BF16),
        ((two, width), F32),
        ((3, two, width), BF16),
        ((2 * pairs, two, rows), BF16),
        ((two, width), BF16),
        ((two, width), F32),
        ((two, hidden), BF16),
        ((two, hidden), BF16),
        ((tokens, width), BF16),
        ((2, width, two), BF16),
        ((width, rows), BF16),
        ((width, two), BF16),
        (gain.shape, BF16),
        ((16, 128), BF16),
        ((rows, width), BF16),
        ((two, width), BF16),
    ]
    outs = pl.pallas_call(
        functools.partial(forward_kernel, names, dims),
        out_shape=shapes,
        in_specs=[ANY] * (count + 4) + [SMEM, SMEM],
        out_specs=[ANY] * count + [VMEM, VMEM] + [ANY] * len(names),
        scratch_shapes=[pltpu.VMEM(s, t) for s, t in scratch]
        + [
            pltpu.SemaphoreType.DMA((copies,)),
            pltpu.SemaphoreType.DMA((copies,)),
            pltpu.SemaphoreType.DMA((5 + 3 * count + len(names),)),
        ],
        compiler_params=pltpu.CompilerParams(
            collective_id=0, has_side_effects=True, vmem_limit_bytes=60 << 20
        ),
        name="gather_and_forward",
    )(*own, gain, latents, inputs, cotangent, counts, flags)
    full, (norm_gain, result) = outs[:count], outs[count : count + 2]
    return full, norm_gain, result, dict(zip(names, outs[count + 2 :]))


def norm_back(values, gain_row, gradient):
    unit, inverse = normed(values)
    scaled = gradient * gain_row
    grad = inverse * (
        scaled
        - jnp.mean(scaled, axis=-1, keepdims=True)
        - unit * jnp.mean(scaled * unit, axis=-1, keepdims=True)
    )
    return grad, jnp.sum(gradient * unit, axis=0, keepdims=True)


def attention_back(q, k, v, out_grad, prob, delta):
    prob_grad = dot_nt(out_grad, v)
    weight = prob.astype(F32)
    if delta is None:
        delta = jnp.sum(weight * prob_grad, axis=-1, keepdims=True)
    score_grad = low(weight * (prob_grad - delta))
    q_grad = join_heads(dot(score_grad, k)) * 0.125
    k_grad = low(dot(q.T, score_grad) * 0.125).T
    v_grad = low(dot(out_grad.T, prob)).T
    return low(q_grad), k_grad, v_grad


def add_blocks(total, where, part, there):
    total[where] = (total[where].astype(F32) + part[there].astype(F32)).astype(BF16)


def backward_kernel(names, dims, *refs):
    rows, tokens, width, hidden = dims
    two, quarter, pairs = 2 * rows, hidden // 4, width // 128
    count = 6
    halves, ring = 2 * count, 3
    order = (5, 4, 3, 2, 1, 0)
    refs = list(refs)

    def take(n):
        out = refs[:n]
        del refs[:n]
        return out

    full = take(count)
    gain, lat, cot, flags = take(4)
    kept = dict(zip(names, take(len(names))))
    outs = take(count)
    gain_out, lat_grad, dx = take(3)
    total = take(count)
    from_y, from_x = take(ring), take(ring)
    from_a, from_b, from_c, from_d, from_z, end_c, end_d = (take(halves) for _ in range(7))
    by_c, by_d, by_z = (take(halves) for _ in range(3))
    wr, wt, grad_ac, du_sib, r_sib, ge_sib, dcu_sib, rs_sib, dkv_sib = take(9)
    gain_acc, gain_sub, gain_dp, send, recv, local, free = take(7)
    place = Place()
    x, y, z, c = place.x, place.y, place.z, place.c
    sems = Sems(place, send, recv)
    local_count = [0]

    def local_copy(src, dst):
        made = pltpu.make_async_copy(src, dst, local.at[local_count[0]])
        local_count[0] += 1
        made.start()
        return made

    me_dp, me_sub = z * 2 + y, x * 2 + c
    sub_peers = [(me_dp, (me_sub + k) % 4) for k in (1, 2, 3)]
    dp_peers = [((me_dp + k) % 8, me_sub) for k in range(1, 8)]
    px, py, pc = place.dev(x=1 - x), place.dev(y=1 - y), place.dev(c=1 - c)
    first_live = flags[0] == 0
    gain_acc[...] = jnp.zeros_like(gain_acc)

    ones, twos, threes = {}, {}, {}
    block_rows, block_columns = total[0].shape[4:]

    def where(i):
        return total[order[i // 2]], i % 2

    def clear():
        for into in (*from_c, *from_d, *from_z):

            @pl.when(z == 0)
            def _():
                into[0] = jnp.zeros(into.shape[1:], BF16)

            @pl.when(z == 3)
            def _():
                into[2] = jnp.zeros(into.shape[1:], BF16)

    def step_one(i):
        a, h = where(i)
        if i >= ring:
            pl.semaphore_wait(free.at[i - ring], 2)
        ones[i] = [
            sems.copy(a.at[h, :, :, 1 - y, piece("CA", block_rows)], from_y[i % ring], py),
            sems.copy(a.at[h, 1 - x, :, :, piece("BD", block_rows)], from_x[i % ring], px),
        ]

    def step_two(i):
        a, h = where(i)
        wait_all(ones.pop(i))
        ca, bd = piece("CA", block_rows), piece("BD", block_rows)
        pa, pb, pc_, pd = (piece(n, block_rows) for n in ("A", "B", "C", "D"))
        fy, fx = from_y[i % ring], from_x[i % ring]

        @pl.loop(0, 8)
        def _(j):
            add_blocks(a, (h, j // 4, j % 4, y, ca), fy, (j // 4, j % 4))
            add_blocks(a, (h, x, j // 2, j % 2, bd), fx, (j // 2, j % 2))

        if i + ring < halves:
            for device in (px, py):
                pl.semaphore_signal(free.at[i], inc=1, device_id=device, device_id_type=MESH_ID)
        collect_c = Collect(sems, lambda o: a.at[h, :, o, y, pc_], from_c[i], by_c[i])
        collect_d = Collect(sems, lambda o: a.at[h, x, o, :, pd], from_d[i], by_d[i])
        got = [
            sems.copy(a.at[h, 1 - x, :, y, pa], from_a[i], px),
            sems.copy(a.at[h, x, :, 1 - y, pb], from_b[i], py),
        ]
        twos[i] = (collect_c, collect_d, got)

    def step_two_forward(i):
        a, h = where(i)
        pc_, pd = piece("C", block_rows), piece("D", block_rows)

        def add_c(o):
            for j in range(2):
                add_blocks(a, (h, j, o, y, pc_), by_c[i], j)

        def add_d(o):
            for j in range(2):
                add_blocks(a, (h, x, o, j, pd), by_d[i], j)

        twos[i][0].part = lambda o: a.at[h, :, o, y, pc_]
        twos[i][1].part = lambda o: a.at[h, x, o, :, pd]
        twos[i][0].forward(add_c)
        twos[i][1].forward(add_d)

    def step_three(i):
        a, h = where(i)
        collect_c, collect_d, got = twos.pop(i)
        collect_c.finish()
        collect_d.finish()
        wait_all(got)
        pa, pb, pc_, pd = (piece(n, block_rows) for n in ("A", "B", "C", "D"))
        fc, fd = from_c[i], from_d[i]

        @pl.loop(0, 4)
        def _(j):
            add_blocks(a, (h, x, j, y, pa), from_a[i], j)
            add_blocks(a, (h, x, j, y, pb), from_b[i], j)

        @pl.loop(0, 2)
        def _(j):
            a[h, j, z, y, pc_] = low(
                a[h, j, z, y, pc_].astype(F32)
                + fc[0, j].astype(F32)
                + fc[1, j].astype(F32)
                + fc[2, j].astype(F32)
            )
            a[h, x, z, j, pd] = low(
                a[h, x, z, j, pd].astype(F32)
                + fd[0, j].astype(F32)
                + fd[1, j].astype(F32)
                + fd[2, j].astype(F32)
            )

        ab = piece("AB", block_rows)
        collect = Collect(sems, lambda o: a.at[h, x, o, y, ab], from_z[i], by_z[i])
        got = [
            sems.copy(a.at[h, 1 - x, z, y, pc_], end_c[i], px),
            sems.copy(a.at[h, x, z, 1 - y, pd], end_d[i], py),
        ]
        threes[i] = (collect, got)

    def step_three_forward(i):
        a, h = where(i)
        ab = piece("AB", block_rows)
        collect = threes[i][0]
        collect.part = lambda o: a.at[h, x, o, y, ab]
        collect.forward(lambda o: add_blocks(a, (h, x, o, y, ab), by_z[i], ...))

    def step_four(i):
        a, h = where(i)
        collect, got = threes.pop(i)
        collect.finish()
        wait_all(got)
        fz, o = from_z[i], outs[order[i // 2]]
        if o.shape[0] == block_rows:
            first, columns = 0, pl.ds(h * block_columns, block_columns)
        else:
            first, columns = h * block_rows, slice(None)

        def put(name, value):
            at = piece(name, block_rows)
            o[pl.ds(first + at.start, at.size), columns] = (
                a[h, x, z, y, at].astype(F32) + value
            )

        put("AB", fz[0].astype(F32) + fz[1].astype(F32) + fz[2].astype(F32))
        put("C", end_c[i][...].astype(F32))
        put("D", end_d[i][...].astype(F32))

    run_step = {
        "1": step_one,
        "2": step_two,
        "g": step_two_forward,
        "3": step_three,
        "f": step_three_forward,
        "4": step_four,
    }
    places = {"1": 0, "2": 1, "g": 2, "3": 3, "f": 4, "4": 5}
    steps = collections.deque(slots(halves, places, "12g3f4"))
    ready = [0]

    def advance(n):
        while n > 0 and steps and (steps[0][1] != "1" or steps[0][2] < ready[0]):
            unused, name, i = steps.popleft()
            run_step[name](i)
            n -= 1

    def done(m):
        ready[0] += 2
        advance(2)

    def square_grad(m, at, products):
        size = 4 * block_rows

        @pl.loop(0, 2)
        def _(n):
            rows_at = pl.ds(pl.multiple_of(n * size, size), size)
            value = None
            for left, right in products:
                term = dot(left[rows_at], right())
                value = term if value is None else value + term
            for h in range(2):
                part = low(value[:, h * block_columns : (h + 1) * block_columns])
                total[m][h, at, pl.ds(n * 2, 2)] = part.reshape(2, 2, block_rows, block_columns)

    def put_hidden(m, h, zz, value):
        for yy in range(2):
            part = value[:, yy * block_columns : (yy + 1) * block_columns]
            total[m][h, :, zz, yy] = low(part).reshape(2, block_rows, block_columns)

    def hidden_grad(m, h, left, right):
        @pl.loop(0, 4)
        def _(zz):
            put_hidden(m, h, zz, dot(left, right[:, lanes(zz, quarter)]))

    def both(own, other):
        return jnp.concatenate([own, other], axis=0)

    def send_off(src, dst):
        return sems.copy(src, dst, pc, later=False)

    def pick(first, second):
        return jnp.where(first_live, first, second)

    def back_through(into, act, blocks):
        into[...] = jnp.zeros_like(into)

        @pl.loop(0, blocks)
        def _(s):
            into[...] += dot_nt(act[s // 2, s % 2], square_block(wr, s // 2, s % 2))

    def self_part(mh, gps, gyt, mnt, sbt, l1t, du, r, cot_v, aa, ac, sqkv, sp, grad_aa, out_grad):
        loads = {
            name: local_copy(src, dst)
            for name, src, dst in (
                ("gyt", kept["gyt"], gyt),
                ("mh", kept["mh"], mh),
                ("wt", full[5], wt),
                ("cot", cot, cot_v),
                ("gps", kept["gps"], gps),
                ("wr", full[4], wr),
                ("aa", kept["aa"], aa),
                ("mnt", kept["mnt"], mnt),
                ("sqkv", kept["sqkv"], sqkv),
                ("sp", kept["sp"], sp),
                ("ac", kept["ac"], ac),
                ("sbt", kept["sbt"], sbt),
                ("l1t", kept["l1t"], l1t),
            )
        }
        clear()
        greet(place, sub_peers + dp_peers)
        loads["gyt"].wait()
        loads["mh"].wait()
        for h in range(2):
            left = gyt[:, h * block_rows : (h + 1) * block_rows]
            left = left.reshape(2 * block_rows, 2 * two)
            hidden_grad(5, h, left, mh)
            ready[0] += 1
            advance(1)

        for name in ("wt", "cot", "gps"):
            loads[name].wait()
        for at, value in (
            (pl.ds(0, rows), pick(cot_v[0], cot_v[1])),
            (pl.ds(rows, rows), pick(cot_v[1], cot_v[0])),
        ):
            grad_aa[at] = value
        out_grad[...] = low(grad_aa[...])

        @pl.loop(0, 4)
        def _(s):
            grad = dot(out_grad[...], hidden_block(wt, s))
            du[s // 2, s % 2] = low(grad * gps[:, lanes(s, quarter)].astype(F32))

        sent = send_off(du.at[:, 1 - c], du_sib)
        advance(2)
        for name in ("wr", "aa", "mnt"):
            loads[name].wait()
        back_through(grad_ac, du, 4)
        grad, gain_row = norm_back(aa[...], gain[4:5], grad_ac[...])
        grad_aa[...] += grad
        gain_acc[0, 4:5] = gain_row
        advance(2)
        next_wr = local_copy(full[3], wr)
        next_wt = local_copy(full[2], wt)
        sent.wait_recv()

        @pl.loop(0, 2)
        def _(a):
            square_grad(4, a, [(mnt, lambda: both(du[a, c], du_sib[a]))])

        done(4)

        r[1, 1] = low(grad_aa[...])
        for made in (next_wr, loads["sqkv"], loads["sp"], loads["ac"], loads["sbt"], loads["l1t"]):
            made.wait()
        out_grad[...] = low(dot_nt(r[1, 1], square_block(wr, 1, 1)))

        advance(2)
        for part in range(2):

            @pl.loop(part * pairs, (part + 1) * pairs, unroll=3)
            def _(i):
                at, row_at = lanes(i % pairs, 128), lanes(i // pairs, rows)
                r[0, 0, row_at, at], r[0, 1, row_at, at], r[1, 0, row_at, at] = attention_back(
                    stack_heads(sqkv[0, row_at, at]),
                    sqkv[1, row_at, at],
                    sqkv[2, row_at, at],
                    stack_heads(out_grad[row_at, at]),
                    sp[i],
                    None,
                )

            advance(2)

        sent_r = send_off(r.at[:, 1 - c], r_sib)
        back_through(grad_ac, r, 3)
        grad, gain_row = norm_back(ac[...], gain[3:4], grad_ac[...])
        grad_ac[...] = grad_aa[...] + grad
        gain_acc[0, 3:4] = gain_row
        advance(2)
        sent_r.wait_recv()
        square_grad(3, 0, [(sbt, lambda: both(r[0, c], r_sib[0]))])
        square_grad(3, 1, [(l1t, lambda: both(r[1, c], r_sib[1]))])
        done(3)
        sent.wait_send()
        sent_r.wait_send()
        next_wt.wait()

    def cross_part(
        ch, gpc, ge, cnt, du, mid, lst, rs, xbt, kv, cp, cq, co, dco, xl, dxs, lat_v, grad_mid
    ):
        loads = {
            name: local_copy(src, dst)
            for name, src, dst in (
                ("ch", kept["ch"], ch),
                ("gpc", kept["gpc"], gpc),
                ("wr", full[1], wr),
                ("mid", kept["mid"], mid),
                ("cnt", kept["cnt"], cnt),
                ("cq", kept["cq"], cq),
                ("co", kept["co"], co),
                ("kv", kept["kv"], kv),
                ("cp", kept["cp"], cp),
                ("lst", kept["lst"], lst),
                ("xbt", kept["xbt"], xbt),
                ("lat", lat, lat_v),
            )
        }
        for i in range(2):
            lat_grad_dead = grad_ac[rows:]
            lat_grad[i] = lat_grad_dead
        low_grad = low(grad_ac[:rows])
        ge[...] = low_grad.T.reshape(2, 2, width // 4, rows)
        sent = [send_off(ge.at[:, 1 - c], ge_sib)]
        loads["gpc"].wait()
        dco[...] = low_grad

        @pl.loop(0, 4)
        def _(s):
            grad = dot(dco[...], hidden_block(wt, s))
            du[s // 2, s % 2] = low(grad * gpc[:, lanes(s, quarter)].astype(F32))

        sent.append(send_off(du.at[:, 1 - c], dcu_sib))
        advance(2)
        loads["ch"].wait()
        sent[0].wait_recv()
        for h in range(2):
            at = pl.ds(h * block_rows, block_rows)
            left = [g.reshape(2 * block_rows, rows) for g in (ge[:, c, at], ge_sib[:, at])]
            hidden_grad(2, h, jnp.concatenate(left, axis=1), ch)
        done(2)

        for name in ("wr", "mid", "cnt"):
            loads[name].wait()
        back_through(grad_mid, du, 4)
        grad, gain_row = norm_back(mid[...], gain[2:3], grad_mid[...])
        grad_mid[...] = grad_ac[:rows] + grad
        gain_acc[0, 2:3] = gain_row
        advance(2)
        next_wr = local_copy(full[0], wr)
        sent[1].wait_recv()

        @pl.loop(0, 2)
        def _(a):
            square_grad(1, a, [(cnt, lambda: both(du[a, c], dcu_sib[a]))])

        done(1)

        rs[1] = low(grad_mid[...])
        next_wr.wait()
        dco[...] = low(dot_nt(rs[1], square_block(wr, 1, 1)))
        for name in ("cq", "co", "kv", "cp"):
            loads[name].wait()

        advance(2)
        for part in range(3):

            @pl.loop(part * pairs // 3, (part + 1) * pairs // 3, unroll=2)
            def _(p):
                at = lanes(p, 128)
                out_grad = stack_heads(dco[:, at])
                attended = co[:, at]
                delta = jnp.sum(
                    out_grad.astype(F32) * both(attended, attended), axis=-1, keepdims=True
                )
                rs[0, :, at], kv[0, :, at], kv[1, :, at] = attention_back(
                    stack_heads(cq[:, at]), kv[0, :, at], kv[1, :, at], out_grad, cp[p], delta
                )

            advance(2)

        sent.append(send_off(rs.at[1 - c], rs_sib))
        sent.append(send_off(kv.at[c], dkv_sib))
        advance(2)
        for name in ("lst", "xbt", "lat"):
            loads[name].wait()
        sent[2].wait_recv()
        sent[3].wait_recv()
        square_grad(0, c, [(lst, lambda: both(rs[c], rs_sib[...]))])
        own_tokens, their_tokens = (xbt.at[:, pl.ds(n * tokens, tokens)] for n in range(2))
        square_grad(
            0,
            1 - c,
            [(own_tokens, lambda: kv[1 - c]), (their_tokens, lambda: dkv_sib[...])],
        )
        done(0)

        grad, gain_row = norm_back(
            pick(lat_v[0], lat_v[1]), gain[0:1], dot_nt(rs[0], square_block(wr, 0, 0))
        )
        gain_acc[0, 0:1] = gain_row
        live_grad = grad_mid[...] + grad
        lat_grad[0] = pick(live_grad, lat_grad[0])
        lat_grad[1] = pick(lat_grad[1], live_grad)
        advance(2)
        out = []
        parts = tokens // 256

        def fetch(n):
            return [
                local_copy(kept["xl"].at[pl.ds(n * 256 + i * 128, 128)], xl.at[i]) for i in range(2)
            ]

        fetched = fetch(0)
        for n in range(parts):
            for made in fetched + out:
                made.wait()

            @pl.loop(0, 2)
            def _(i):
                at = pl.ds(pl.multiple_of(n * 256 + i * 128, 128), 128)
                term = dot_nt(kv[0, at], square_block(wr, 0, 1))
                term += dot_nt(kv[1, at], square_block(wr, 1, 0))
                grad, gain_row = norm_back(xl[i].astype(F32), gain[1:2], term)
                dxs[i] = grad
                gain_acc[0, 1:2] += gain_row

            if n + 1 < parts:
                fetched = fetch(n + 1)
            out = [
                local_copy(dxs.at[i], dx.at[pl.ds(n * 256 + i * 128, 128)]) for i in range(2)
            ]
            advance(3)
        for made in out:
            made.wait()
        gain_one = [sems.copy(gain_acc.at[0], spot(gain_sub, k), sub_peers[k]) for k in range(3)]
        advance(3)
        wait_all(gain_one)
        gain_acc[1] = gain_acc[0] + gain_sub[0] + gain_sub[1] + gain_sub[2]
        gain_two = [sems.copy(gain_acc.at[1], spot(gain_dp, k), dp_peers[k]) for k in range(7)]
        for made in sent:
            made.wait_send()
        return gain_two

    def vmem(*shape, dtype=BF16):
        return pltpu.VMEM(shape, dtype)

    holder = {}

    pl.run_scoped(
        self_part,
        vmem(2 * two, hidden),
        vmem(two, hidden),
        vmem(2, width // 4, 2 * two),
        vmem(width, 2 * two),
        vmem(width, 2 * two),
        vmem(width, 2 * two),
        vmem(2, 2, two, quarter),
        vmem(2, 2, two, width),
        vmem(2, rows, width, dtype=F32),
        vmem(two, width, dtype=F32),
        vmem(two, width, dtype=F32),
        vmem(3, two, width),
        vmem(2 * pairs, two, rows),
        vmem(two, width, dtype=F32),
        vmem(two, width),
    )

    def run_cross(*bufs):
        holder["gain"] = cross_part(*bufs)

    pl.run_scoped(
        run_cross,
        vmem(two, hidden),
        vmem(rows, hidden),
        vmem(2, 2, width // 4, rows),
        vmem(width, two),
        vmem(2, 2, rows, quarter),
        vmem(rows, width, dtype=F32),
        vmem(width, two),
        vmem(2, rows, width),
        vmem(width, 2 * tokens),
        vmem(2, tokens, width),
        vmem(pairs, two, tokens),
        vmem(rows, width),
        vmem(rows, width, dtype=F32),
        vmem(rows, width),
        vmem(2, 128, width),
        vmem(2, 128, width, dtype=F32),
        vmem(2, rows, width, dtype=F32),
        vmem(rows, width, dtype=F32),
    )
    advance(len(steps))
    wait_all(holder["gain"])
    gain_out[...] = gain_acc[1] + jnp.sum(gain_dp[...], axis=0)
    sems.drain()


def backward_all(shard, full, norm_gain, latents, cotangent, flags, kept):
    count = len(full)
    rows, width = latents.shape[1:]
    tokens, hidden = kept["xl"].shape[0], kept["mh"].shape[1]
    dims = (rows, tokens, width, hidden)
    two = 2 * rows
    copies = 10 + 6 + 2 * count * (2 + 10 + 6)
    ring, halves = 3, 2 * count
    block_rows, block_columns = full[0].shape[5:]

    def room(number, lead, sixths):
        return [pltpu.VMEM(lead + (block_rows * sixths // 6, block_columns), BF16)] * number

    scratch = [pltpu.VMEM((2,) + full[0].shape[2:], BF16)] * count
    scratch += room(ring, (2, 4), 3) + room(ring, (4, 2), 3)
    scratch += room(halves, (4,), 1) + room(halves, (4,), 1)
    scratch += room(halves, (3, 2), 2) + room(halves, (3, 2), 2) + room(halves, (3,), 2)
    scratch += room(halves, (), 2) + room(halves, (), 2)
    scratch += room(halves, (2,), 2) + room(halves, (2,), 2) + room(halves, (), 2)
    scratch += [
        pltpu.VMEM(full[0].shape, BF16),
        pltpu.VMEM(full[2].shape, BF16),
        pltpu.VMEM((two, width), F32),
        pltpu.VMEM((2, two, hidden // 4), BF16),
        pltpu.VMEM((2, two, width), BF16),
        pltpu.VMEM((2, width // 4, rows), BF16),
        pltpu.VMEM((2, rows, hidden // 4), BF16),
        pltpu.VMEM((rows, width), BF16),
        pltpu.VMEM((tokens, width), BF16),
        pltpu.VMEM((2, 8, width), F32),
        pltpu.VMEM((3, 8, width), F32),
        pltpu.VMEM((7, 8, width), F32),
        pltpu.SemaphoreType.DMA((copies,)),
        pltpu.SemaphoreType.DMA((copies,)),
        pltpu.SemaphoreType.DMA((48,)),
        pltpu.SemaphoreType.REGULAR((halves - ring,)),
    ]
    shapes = [jax.ShapeDtypeStruct(d, F32) for d in shard]
    shapes += [
        jax.ShapeDtypeStruct((8, width), F32),
        jax.ShapeDtypeStruct(latents.shape, F32),
        jax.ShapeDtypeStruct((tokens, width), F32),
    ]
    outs = pl.pallas_call(
        functools.partial(backward_kernel, tuple(kept), dims),
        out_shape=shapes,
        in_specs=[ANY] * count + [VMEM, ANY, ANY, SMEM] + [ANY] * len(kept),
        out_specs=[VMEM] * (count + 2) + [ANY],
        scratch_shapes=scratch,
        compiler_params=pltpu.CompilerParams(
            collective_id=1, has_side_effects=True, vmem_limit_bytes=60 << 20
        ),
        name="backward_and_scatter",
    )(*full, norm_gain, latents, cotangent, flags, *kept.values())
    return outs[:count], *outs[count:]


def finish_kernel(gain_share, gain_rows, count, *refs):
    flags, result, lat_grad, tok_grad, gain_total = refs[:5]
    shards_in = refs[5 : 5 + count]
    out_result, out_lat, out_tok, out_gain = refs[5 + count : 9 + count]
    shards_out = refs[9 + count : 9 + 2 * count]
    gain_in, zeros, sems_in, sems_out = refs[9 + 2 * count : 13 + 2 * count]
    held = refs[13 + 2 * count :]
    tokens, pieces = tok_grad.shape[0], held[-1].shape[0]
    size = tokens // pieces
    live = jnp.where(flags[0] == 0, 0, 1)
    moves = []
    for n in range(pieces):
        at = pl.ds(n * size, size)
        moves.append((tok_grad.at[at], held[-1].at[n], out_tok.at[live, at]))
    moves += zip((result, lat_grad, *shards_in), held, (out_result, out_lat, *shards_out))
    gain_copy = pltpu.make_async_copy(gain_total, gain_in, sems_in.at[len(moves)])
    reads = [
        pltpu.make_async_copy(src, room, sems_in.at[i]) for i, (src, room, dst) in enumerate(moves)
    ]
    for made in reads:
        made.start()
    gain_copy.start()
    zeros[...] = jnp.zeros_like(zeros)
    started = []
    for n in range(pieces):
        started.append(
            pltpu.make_async_copy(
                zeros, out_tok.at[1 - live, pl.ds(n * size, size)], sems_out.at[len(moves) + n]
            )
        )
        started[-1].start()
    for i, (src, room, dst) in enumerate(moves):
        reads[i].wait()
        started.append(pltpu.make_async_copy(room, dst, sems_out.at[i]))
        started[-1].start()
    gain_copy.wait()
    dp = lax.axis_index("dp")
    for i in range(8):

        @pl.when(dp == i)
        def _():
            out_gain[...] = gain_in[:gain_rows, i * gain_share : (i + 1) * gain_share]

    for made in started:
        made.wait()


def finish_all(gain_shape, flags, result, lat_grad, tok_grad, gain_total, shards_in):
    count, pieces = len(shards_in), 4
    tokens, width = tok_grad.shape
    arrays = [result, lat_grad, tok_grad, gain_total, *shards_in]
    shapes = [
        jax.ShapeDtypeStruct(result.shape, F32),
        jax.ShapeDtypeStruct(lat_grad.shape, F32),
        jax.ShapeDtypeStruct((2, tokens, width), F32),
        jax.ShapeDtypeStruct(gain_shape, F32),
    ]
    shapes += [jax.ShapeDtypeStruct(a.shape, F32) for a in shards_in]
    return pl.pallas_call(
        functools.partial(finish_kernel, gain_shape[1], gain_shape[0], count),
        out_shape=shapes,
        in_specs=[SMEM] + [ANY] * len(arrays),
        out_specs=[ANY] * 3 + [VMEM] + [ANY] * count,
        scratch_shapes=[
            pltpu.VMEM(gain_total.shape, F32),
            pltpu.VMEM((tokens // pieces, width), F32),
            pltpu.SemaphoreType.DMA((3 + count + pieces,)),
            pltpu.SemaphoreType.DMA((2 + count + 2 * pieces,)),
            *(pltpu.VMEM(a.shape, F32) for a in (result, lat_grad, *shards_in)),
            pltpu.VMEM((pieces, tokens // pieces, width), F32),
        ],
        compiler_params=pltpu.CompilerParams(vmem_limit_bytes=60 << 20),
        name="write_outputs",
    )(flags, *arrays)


def layer_norm(values, gain_row):
    centred = values - jnp.mean(values, axis=-1, keepdims=True)
    inverse = lax.rsqrt(jnp.mean(centred * centred, axis=-1, keepdims=True) + EPSILON)
    return centred * inverse * gain_row


def norm_backward(values, gain_row, gradient):
    unused, pull_back = jax.vjp(layer_norm, values, gain_row)
    return pull_back(gradient)


def gelu_tanh(values):
    return jax.nn.gelu(values, approximate=True)


def mm(left_side, weight):
    return jnp.dot(left_side, weight, preferred_element_type=F32)


def mm_nt(left_side, weight):
    return lax.dot_general(left_side, weight, (((1,), (1,)), ((), ())), preferred_element_type=F32)


def mm_tn(left_side, gradient):
    return lax.dot_general(
        left_side, gradient, (((0,), (0,)), ((), ())), preferred_element_type=F32
    )


def low(values):
    return values.astype(BF16)


def heads_of(values):
    return values.reshape(values.shape[:-1] + (HEADS, values.shape[-1] // HEADS))


def mlp_forward(residual, gain_row, up, down_t):
    normed = low(layer_norm(residual, gain_row))
    pre_act = mm(normed, up)
    hidden = low(gelu_tanh(pre_act))
    return normed, pre_act, hidden, mm_nt(hidden, down_t)


def mlp_backward(residual, gain_row, normed, pre_act, hidden, up, down_t, grad_out):
    grad_low = low(grad_out)
    grad_down_t = mm_tn(grad_low, hidden)
    grad_hidden = mm(grad_low, down_t)
    unused, gelu_back = jax.vjp(gelu_tanh, pre_act)
    grad_pre = low(gelu_back(grad_hidden)[0])
    grad_up = mm_tn(normed, grad_pre)
    grad_resid, grad_gain = norm_backward(residual, gain_row, mm_nt(grad_pre, up))
    return grad_resid, grad_gain, grad_up, grad_down_t


def live_layer(live_lat, dead_lat, tokens, count, live_cot, dead_cot, weights, norm_gain):
    c_attn, c_up, c_down_t, s_attn, s_up, s_down_t = weights
    rows, width = live_lat.shape
    scale = (width // HEADS) ** (-0.5)
    lat_low = low(layer_norm(live_lat, norm_gain[0]))
    queries = low(mm(lat_low, c_attn[:, :width]))
    token_values = tokens.astype(F32)
    tok_low = low(layer_norm(token_values, norm_gain[1]))
    kv_weight = c_attn[:, width : 3 * width]
    key_value = low(mm(tok_low, kv_weight))
    keys, values = heads_of(key_value[:, :width]), heads_of(key_value[:, width:])
    scores = (
        jnp.einsum("qhd,khd->hqk", heads_of(queries), keys, preferred_element_type=F32) * scale
    )
    valid = (jnp.arange(tokens.shape[0]) < count)[None, None, :]
    probs = jax.nn.softmax(jnp.where(valid, scores, MASKED), axis=-1)
    probs_low = low(probs)
    attended = jnp.einsum("hqk,khd->qhd", probs_low, values, preferred_element_type=F32)
    attended = attended.reshape(rows, width)
    cross_low = low(attended)
    middle = live_lat + mm(cross_low, c_attn[:, 3 * width :])
    c_norm, c_pre, c_hidden, c_mlp = mlp_forward(middle, norm_gain[2], c_up, c_down_t)
    after_cross = jnp.concatenate([middle + c_mlp, dead_lat], axis=0)

    self_low = low(layer_norm(after_cross, norm_gain[3]))
    qkv = low(mm(self_low, s_attn[:, : 3 * width])).reshape(2, rows, 3 * width)
    s_q = heads_of(qkv[..., :width])
    s_k = heads_of(qkv[..., width : 2 * width])
    s_v = heads_of(qkv[..., 2 * width :])
    s_scores = jnp.einsum("iqhd,ikhd->ihqk", s_q, s_k, preferred_element_type=F32) * scale
    s_probs = jax.nn.softmax(s_scores, axis=-1)
    s_probs_low = low(s_probs)
    s_out = jnp.einsum("ihqk,ikhd->iqhd", s_probs_low, s_v, preferred_element_type=F32)
    s_out_low = low(s_out.reshape(2 * rows, width))
    after_attn = after_cross + mm(s_out_low, s_attn[:, 3 * width :])
    m_norm, m_pre, m_hidden, m_mlp = mlp_forward(after_attn, norm_gain[4], s_up, s_down_t)
    result = after_attn + m_mlp

    cotangent = jnp.concatenate([live_cot, dead_cot], axis=0)
    grad_in, gain_four, d_s_up, d_s_down_t = mlp_backward(
        after_attn, norm_gain[4], m_norm, m_pre, m_hidden, s_up, s_down_t, cotangent
    )
    grad_attn = cotangent + grad_in
    grad_y = low(grad_attn)
    d_s_o = mm_tn(s_out_low, grad_y)
    grad_out = heads_of(low(mm_nt(grad_y, s_attn[:, 3 * width :])).reshape(2, rows, width))
    grad_probs = jnp.einsum("iqhd,ikhd->ihqk", grad_out, s_v, preferred_element_type=F32)
    delta = jnp.sum(grad_probs * s_probs, axis=-1, keepdims=True)
    grad_scores = low(s_probs * (grad_probs - delta))
    g_q = jnp.einsum("ihqk,ikhd->iqhd", grad_scores, s_k, preferred_element_type=F32) * scale
    g_k = jnp.einsum("ihqk,iqhd->ikhd", grad_scores, s_q, preferred_element_type=F32) * scale
    g_v = jnp.einsum("ihqk,iqhd->ikhd", s_probs_low, grad_out, preferred_element_type=F32)
    grad_qkv = low(
        jnp.concatenate([g.reshape(2 * rows, width) for g in (g_q, g_k, g_v)], axis=-1)
    )
    d_s_qkv = mm_tn(self_low, grad_qkv)
    grad_in, gain_three = norm_backward(
        after_cross, norm_gain[3], mm_nt(grad_qkv, s_attn[:, : 3 * width])
    )
    grad_cross = grad_attn + grad_in
    live_grad, dead_grad = grad_cross[:rows], grad_cross[rows:]
    grad_in, gain_two, d_c_up, d_c_down_t = mlp_backward(
        middle, norm_gain[2], c_norm, c_pre, c_hidden, c_up, c_down_t, live_grad
    )
    grad_middle = live_grad + grad_in
    grad_cross_y = low(grad_middle)
    d_c_o = mm_tn(cross_low, grad_cross_y)
    grad_cross_out = low(mm_nt(grad_cross_y, c_attn[:, 3 * width :]))
    out_heads = heads_of(grad_cross_out)
    grad_weights = jnp.einsum("qhd,khd->hqk", out_heads, values, preferred_element_type=F32)
    row_delta = jnp.transpose(jnp.sum(heads_of(grad_cross_out.astype(F32) * attended), axis=-1))
    grad_scores = low(probs * (grad_weights - row_delta[..., None]))
    grad_query = low(
        (
            jnp.einsum("hqk,khd->qhd", grad_scores, keys, preferred_element_type=F32) * scale
        ).reshape(rows, width)
    )
    grad_keys = (
        jnp.einsum("hqk,qhd->khd", grad_scores, heads_of(queries), preferred_element_type=F32)
        * scale
    )
    grad_values = jnp.einsum("hqk,qhd->khd", probs_low, out_heads, preferred_element_type=F32)
    grad_kv = low(
        jnp.concatenate(
            [grad_keys.reshape(-1, width), grad_values.reshape(-1, width)], axis=-1
        )
    )
    d_c_kv = mm_tn(tok_low, grad_kv)
    grad_tokens, gain_one = norm_backward(token_values, norm_gain[1], mm_nt(grad_kv, kv_weight))
    d_c_q = mm_tn(lat_low, grad_query)
    grad_in, gain_zero = norm_backward(
        live_lat, norm_gain[0], mm_nt(grad_query, c_attn[:, :width])
    )
    live_lat_grad = grad_middle + grad_in
    d_c_attn = low(jnp.concatenate([d_c_q, d_c_kv, d_c_o], axis=1))
    d_s_attn = low(jnp.concatenate([d_s_qkv, d_s_o], axis=1))
    gain_grad = jnp.stack([gain_zero, gain_one, gain_two, gain_three, gain_four])
    grads = (d_c_attn, low(d_c_up), low(d_c_down_t), d_s_attn, low(d_s_up), low(d_s_down_t))
    return result, live_lat_grad, dead_grad, grad_tokens, grads, gain_grad


def column_blocks(blocks):
    sub, dp, rows, columns = blocks.shape
    return blocks.transpose(1, 2, 0, 3).reshape(dp * rows, sub * columns)


def row_blocks(blocks):
    sub, dp, rows, columns = blocks.shape
    return blocks.transpose(0, 2, 1, 3).reshape(sub * rows, dp * columns)


def shards(*arrays, dp_size, sub_size):
    latents, inputs, counts, flags = arrays[:4]
    cross_attn, cross_up, cross_down, self_attn, self_up, self_down, gains, cotangent = arrays[4:]
    width = latents.shape[-1]
    own = (
        cross_attn,
        cross_up,
        jnp.transpose(cross_down),
        self_attn,
        self_up,
        jnp.transpose(self_down),
    )
    live = jnp.where(flags[0] == 0, 0, 1)
    here = (jnp.arange(inputs.shape[0]) == live)[:, None, None]
    if dp_size == 8 and sub_size == 4:
        full, norm_gain, result, kept = forward_all(
            own, gains, latents, inputs, cotangent, counts, flags
        )
        owned, gain_total, grad_latents, grad_tokens = backward_all(
            [w.shape for w in own], full, norm_gain, latents, cotangent, flags, kept
        )
        result, grad_latents, grad_inputs, gain_owned, *owned = finish_all(
            gains.shape, flags, result, grad_latents, grad_tokens, gain_total, owned
        )
        owned = [jnp.transpose(g) if i in (2, 5) else g for i, g in enumerate(owned)]
        return (result, grad_latents, grad_inputs, *owned, gain_owned)

    blocks = [lax.all_gather(lax.all_gather(w, "dp", axis=0), "sub", axis=0) for w in own]
    norm_gain = lax.all_gather(gains, "dp", axis=1, tiled=True)
    transposed = (False, False, True, False, False, True)
    weights = [
        row_blocks(b) if flip else column_blocks(b) for b, flip in zip(blocks, transposed)
    ]

    def item(array, index):
        return lax.dynamic_index_in_dim(array, index, 0, keepdims=False)

    result, live_grad, dead_grad, grad_tokens, grads, gain_grad = live_layer(
        item(latents, live),
        item(latents, 1 - live),
        item(inputs, live),
        item(counts, live),
        item(cotangent, live),
        item(cotangent, 1 - live),
        weights,
        norm_gain.astype(F32),
    )

    def both(live_part, dead_part):
        first = jnp.where(live == 0, live_part, dead_part)
        second = jnp.where(live == 0, dead_part, live_part)
        return jnp.stack([first, second])

    rows = latents.shape[1]
    result = both(result[:rows], result[rows:])
    grad_latents = both(live_grad, dead_grad)
    grad_inputs = jnp.where(here, grad_tokens[None], 0.0)

    def blocks_of(grad, shape, flip):
        r, c = shape
        if flip:
            return grad.reshape(sub_size, r, dp_size, c).transpose(0, 2, 1, 3)
        return grad.reshape(dp_size, r, sub_size, c).transpose(2, 0, 1, 3)

    grads = [blocks_of(g, w.shape, flip) for g, w, flip in zip(grads, own, transposed)]
    owned = [lax.psum_scatter(g, "sub", scatter_dimension=0) for g in grads]
    owned = [lax.psum_scatter(g.astype(F32), "dp", scatter_dimension=0) for g in owned]
    gain_owned = lax.psum(gain_grad, "sub")
    gain_owned = lax.psum_scatter(gain_owned, "dp", scatter_dimension=1, tiled=True)
    owned = [jnp.transpose(g) if flip else g for g, flip in zip(owned, transposed)]
    return (result, grad_latents, grad_inputs, *owned, gain_owned)


def solution(mesh):
    item = P(("dp", "sub"), None, None)
    weight = P("dp", "sub")
    gain = P(None, "dp")
    placed = (item, item, P(("dp", "sub")), P()) + (weight,) * 6 + (gain, item)
    return jax.shard_map(
        functools.partial(shards, dp_size=mesh.shape["dp"], sub_size=mesh.shape["sub"]),
        mesh=mesh,
        in_specs=placed,
        out_specs=(item, item, item) + (weight,) * 6 + (gain,),
        check_vma=False,
    )
```

profile of v0, /device:TPU:0, one launch (start us, length us, event | category | flops | bytes accessed | tf_op | source)
XLA Modules:
  0.0 273.0 jit_solution(7909464571126580460)
XLA Ops:
  0.6 134.1 %gather_and_forward.1 = (bf16[2,2,2,4,2,96,384]{6,5,4,3,2,1,0:T(8,128)(2,1)}, bf16[2,2,2,4,2,96,384]{6,5,4,3,2,1,0:T(8,128)(2,1)}, bf16[2,2,2,4,2,96,384]{6,5,4,...) custom-call(bf16[96,768]{1,0:T(8,128)(2,1)} %refs_0_.2, ...), custom_call_target="tpu_custom_call" | custom-call | tf_op jit(solution)/shard_map/gather_and_forward/pallas_call | solution.py:770
  134.8 130.1 %backward_and_scatter.1 = (f32[96,768]{1,0:T(8,128)}, f32[96,768]{1,0:T(8,128)}, f32[192,384]{1,0:T(8,128)}, f32[96,768]{1,0:T(8,128)}, f32[96,768]{1,0:T(8,128)...) custom-call(bf16[2,2,2,4,2,96,384]{6,5,4,3,2,1,0:T(8,128)(2,1)} %get-tuple-element.59.re, ...), custom_call_target="tpu_custom_call" | custom-call | tf_op jit(solution)/shard_map/backward_and_scatter/pallas_call | solution.py:1394
  264.9 8.0 %write_outputs.1 = (f32[2,128,768]{2,1,0:T(8,128)}, f32[2,128,768]{2,1,0:T(8,128)}, f32[2,1024,768]{2,1,0:T(8,128)}, f32[5,96]{1,0:T(8,128)}, f32[96,768]{1,0:T(...) custom-call(s32[2]{0:T(128)} %refs_0_.3, ...), custom_call_target="tpu_custom_call" | custom-call | tf_op jit(solution)/shard_map/write_outputs/pallas_call | solution.py:1466
where the time goes:
time: 274 us; the launch traced here: 273 us
  Pallas kernels  272 us (99%)
    pallas_call x1, Pallas kernels, forward_all(): pl.pallas_call(functools.partial(forward_kernel, names, dims), out_shape=...  134 us
    pallas_call x1, Pallas kernels, backward_all(): pl.pallas_call(functools.partial(backward_kernel, tuple(kept), dims), out...  130 us
    pallas_call x1, Pallas kernels, finish_all(): pl.pallas_call(functools.partial(finish_kernel, gain_shape[1], gain_shape...  7.96 us

commit v1 on v0

--- a/solution.py
+++ b/solution.py
@@ -697,7 +697,7 @@
         "4": step_four,
     }
     places = {"1": -2, "f": -1, "2": 0, "g": 0, "3": 1, "4": 2}
-    for slot, name, i in slots(halves, places, "231fg4"):
+    for slot, name, i in slots(halves, places, "2314fg"):
         steps[name](i)
         if work and work[0][0] <= slot:
             work.popleft()[1]()

time: 274 us -> 268 us (0.978)
  Pallas kernels: 272 us -> 267 us
    pallas_call x1, Pallas kernels: 134 us -> 129 us  [forward_all(): pl.pallas_call(functools.partial(forward_kernel, names, dims), out_shape=...]
where the time goes in v1:
time: 268 us
  Pallas kernels  267 us (100%)
    pallas_call x1, Pallas kernels, backward_all(): pl.pallas_call(functools.partial(backward_kernel, tuple(kept), dims), out...  129 us
    pallas_call x1, Pallas kernels, forward_all(): pl.pallas_call(functools.partial(forward_kernel, names, dims), out_shape=...  129 us
    pallas_call x1, Pallas kernels, finish_all(): pl.pallas_call(functools.partial(finish_kernel, gain_shape[1], gain_shape...  7.96 us

profile of v1, /device:TPU:0, one launch (start us, length us, event | category | flops | bytes accessed | tf_op | source)
XLA Modules:
  0.0 267.6 jit_solution(10665802432209939027)
XLA Ops:
  0.6 129.3 %gather_and_forward.1 = (bf16[2,2,2,4,2,96,384]{6,5,4,3,2,1,0:T(8,128)(2,1)}, bf16[2,2,2,4,2,96,384]{6,5,4,3,2,1,0:T(8,128)(2,1)}, bf16[2,2,2,4,2,96,384]{6,5,4,...) custom-call(bf16[96,768]{1,0:T(8,128)(2,1)} %refs_0_.2, ...), custom_call_target="tpu_custom_call" | custom-call | tf_op jit(solution)/shard_map/gather_and_forward/pallas_call | solution.py:770
  130.0 129.5 %backward_and_scatter.1 = (f32[96,768]{1,0:T(8,128)}, f32[96,768]{1,0:T(8,128)}, f32[192,384]{1,0:T(8,128)}, f32[96,768]{1,0:T(8,128)}, f32[96,768]{1,0:T(8,128)...) custom-call(bf16[2,2,2,4,2,96,384]{6,5,4,3,2,1,0:T(8,128)(2,1)} %get-tuple-element.59.re, ...), custom_call_target="tpu_custom_call" | custom-call | tf_op jit(solution)/shard_map/backward_and_scatter/pallas_call | solution.py:1394
  259.5 8.0 %write_outputs.1 = (f32[2,128,768]{2,1,0:T(8,128)}, f32[2,128,768]{2,1,0:T(8,128)}, f32[2,1024,768]{2,1,0:T(8,128)}, f32[5,96]{1,0:T(8,128)}, f32[96,768]{1,0:T(...) custom-call(s32[2]{0:T(128)} %refs_0_.3, ...), custom_call_target="tpu_custom_call" | custom-call | tf_op jit(solution)/shard_map/write_outputs/pallas_call | solution.py:1466

commit v2 on v1

--- a/solution.py
+++ b/solution.py
@@ -699,7 +699,7 @@
     places = {"1": -2, "f": -1, "2": 0, "g": 0, "3": 1, "4": 2}
     for slot, name, i in slots(halves, places, "2314fg"):
         steps[name](i)
-        if work and work[0][0] <= slot:
+        if work and work[0][0] <= slot and name in "234f":
             work.popleft()[1]()
     while work:
         work.popleft()[1]()
@@ -1453,7 +1453,7 @@
 
 
 def finish_all(gain_shape, flags, result, lat_grad, tok_grad, gain_total, shards_in):
-    count, pieces = len(shards_in), 4
+    count, pieces = len(shards_in), 8
     tokens, width = tok_grad.shape
     arrays = [result, lat_grad, tok_grad, gain_total, *shards_in]
     shapes = [

time: 268 us -> 267 us (level)
  no operation moved by 1% of the time
where the time goes in v2:
time: 267 us
  Pallas kernels  266 us (100%)
    pallas_call x1, Pallas kernels, backward_all(): pl.pallas_call(functools.partial(backward_kernel, tuple(kept), dims), out...  129 us
    pallas_call x1, Pallas kernels, forward_all(): pl.pallas_call(functools.partial(forward_kernel, names, dims), out_shape=...  129 us
    pallas_call x1, Pallas kernels, finish_all(): pl.pallas_call(functools.partial(finish_kernel, gain_shape[1], gain_shape...  7.81 us

profile of v2, /device:TPU:0, one launch (start us, length us, event | category | flops | bytes accessed | tf_op | source)
XLA Modules:
  0.0 266.8 jit_solution(15346864156504031606)
XLA Ops:
  0.6 128.8 %gather_and_forward.1 = (bf16[2,2,2,4,2,96,384]{6,5,4,3,2,1,0:T(8,128)(2,1)}, bf16[2,2,2,4,2,96,384]{6,5,4,3,2,1,0:T(8,128)(2,1)}, bf16[2,2,2,4,2,96,384]{6,5,4,...) custom-call(bf16[96,768]{1,0:T(8,128)(2,1)} %refs_0_.2, ...), custom_call_target="tpu_custom_call" | custom-call | tf_op jit(solution)/shard_map/gather_and_forward/pallas_call | solution.py:770
  129.4 129.4 %backward_and_scatter.1 = (f32[96,768]{1,0:T(8,128)}, f32[96,768]{1,0:T(8,128)}, f32[192,384]{1,0:T(8,128)}, f32[96,768]{1,0:T(8,128)}, f32[96,768]{1,0:T(8,128)...) custom-call(bf16[2,2,2,4,2,96,384]{6,5,4,3,2,1,0:T(8,128)(2,1)} %get-tuple-element.59.re, ...), custom_call_target="tpu_custom_call" | custom-call | tf_op jit(solution)/shard_map/backward_and_scatter/pallas_call | solution.py:1394
  258.8 7.8 %write_outputs.1 = (f32[2,128,768]{2,1,0:T(8,128)}, f32[2,128,768]{2,1,0:T(8,128)}, f32[2,1024,768]{2,1,0:T(8,128)}, f32[5,96]{1,0:T(8,128)}, f32[96,768]{1,0:T(...) custom-call(s32[2]{0:T(128)} %refs_0_.3, ...), custom_call_target="tpu_custom_call" | custom-call | tf_op jit(solution)/shard_map/write_outputs/pallas_call | solution.py:1466
